TPU v7x, 32 devices: a whole 2x2x4 slice. The times are simulated.
32 devices in a mesh: groups: 2 (over x), expert: 16 (over z, y, core).
Axes of the slice: x: 2, y: 2, z: 4, core: 2. Of those that a mesh axis runs over, the one named last changes fastest.
Arguments:
- tokens: bfloat16 [2048, 2048], P(('groups', 'expert')), parts along dimension 0, may hold values from -6 to 6
- expert_ids: int32 [2048, 8], P(('groups', 'expert')), parts along dimension 0, may hold values from 0 to 15, as said below
- gate_weights: float32 [2048, 8], P(('groups', 'expert')), parts along dimension 0, may hold values from 0.05 to 0.5
- w_gate: bfloat16 [16, 2048, 768], P('expert'), may hold values from -0.125 to 0.125
- w_up: bfloat16 [16, 2048, 768], P('expert'), may hold values from -0.125 to 0.125
- w_down: bfloat16 [16, 768, 2048], P('expert'), may hold values from -0.21875 to 0.21875
Outputs:
- mixed: bfloat16 [2048, 2048], P(('groups', 'expert')), parts along dimension 0
There are 2 independent parts, one for each index of `groups`. A program takes and returns all parts, laid end to end along the dimension named above; an argument that names none is the same for every part. Nothing has to cross between parts.
Inputs may be any that keep to these rules, and one draw needn't show every extreme that they name: `expert_ids`: each token names 8 different experts. Exactly 2 experts are named exactly 64 times by the tokens of every device; every other expert is named at most 28 times by the tokens of one device, and in every draw some such expert is named exactly 28 times by the tokens of every device.
All inputs are finite; a program needn't handle non-finite values.
Results may differ from a plain program's by a relative error of at most 0.0057.
Values may be sent and summed in bfloat16 or wider, within the bound.
No kernel may reach another device: no remote copies, remote signals or barrier semaphores. Data moves between devices by JAX's collectives and lax.ppermute only.
A program may use at most 128 MiB of HBM per device.

v0:
```python
import functools

import jax
import jax.numpy as jnp
from jax import lax
from jax.experimental import pallas as pl
from jax.experimental.pallas import tpu as pltpu
from jax.sharding import PartitionSpec as P

LANES = 128
IN_VMEM = pl.BlockSpec(memory_space=pltpu.VMEM)
IN_HBM = pl.BlockSpec(memory_space=pltpu.HBM)
DEPTH_STEP = 512
HIDDEN_STEP = 256
SCOPED_BYTES = 8 * 1024 * 1024
KEPT_BYTES = 32 * 1024 * 1024


def in_hbm(array):
    return pltpu.with_memory_space_constraint(array, pltpu.HBM)


def even_split(size, most):
    part = most
    while size % part:
        part //= 2
    return part


def chip_ring(chips):
    across = max(d for d in range(1, chips + 1) if chips % d == 0 and d * d <= chips)
    down = chips // across
    if across == 1 or down % 2:
        return list(range(chips))
    ring = []
    for row in range(down):
        columns = list(range(1, across))
        ring += [row * across + column for column in (columns if row % 2 == 0 else columns[::-1])]
    return [0] + ring + [row * across for row in range(down - 1, 0, -1)]


def ring_pairs(ring, way):
    count = len(ring)
    pairs = []
    for at, chip in enumerate(ring):
        for core in (0, 1):
            step = way if core == at % 2 else -way
            pairs.append((2 * chip + core, 2 * ring[(at + step) % count] + 1 - core))
    return pairs


def pack_kernel(tokens_ref, ids_ref, gates_ref, out_ref, ids_buf, gates_buf, sems):
    width = tokens_ref.shape[1]
    copies = [
        pltpu.make_async_copy(ids_ref, ids_buf, sems.at[0]),
        pltpu.make_async_copy(gates_ref, gates_buf, sems.at[1]),
        pltpu.make_async_copy(tokens_ref, out_ref.at[:, pl.ds(0, width)], sems.at[2]),
    ]
    for copy in copies:
        copy.start()
    for copy in copies[:2]:
        copy.wait()
    rest = gates_buf[...]
    parts = [ids_buf[...].astype(jnp.float32)]
    for _ in range(3):
        parts.append(rest.astype(jnp.bfloat16).astype(jnp.float32))
        rest = rest - parts[-1]
    stacked = jnp.concatenate(parts, axis=0)
    shape = (stacked.shape[0], out_ref.shape[1] - width)
    unit = lax.broadcasted_iota(jnp.int32, shape, 0) == lax.broadcasted_iota(jnp.int32, shape, 1)
    route = lax.dot_general(
        stacked.astype(jnp.bfloat16),
        unit.astype(jnp.float32).astype(jnp.bfloat16),
        (((0,), (0,)), ((), ())),
        preferred_element_type=jnp.float32,
    )
    out_ref[:, width:] = route.astype(jnp.bfloat16)
    copies[2].wait()


def pack_rows(tokens, expert_ids, gate_weights, made):
    rows, width = tokens.shape
    extra = -(-4 * expert_ids.shape[1] // LANES) * LANES
    ids, gates = expert_ids.T, gate_weights.T
    return pl.pallas_call(
        pack_kernel,
        out_shape=made((rows, width + extra), jnp.bfloat16),
        in_specs=[IN_HBM] * 3,
        out_specs=IN_VMEM,
        scratch_shapes=[
            pltpu.VMEM(ids.shape, ids.dtype),
            pltpu.VMEM(gates.shape, gates.dtype),
            pltpu.SemaphoreType.DMA((3,)),
        ],
        compiler_params=pltpu.CompilerParams(vmem_limit_bytes=SCOPED_BYTES),
    )(in_hbm(tokens), in_hbm(ids), in_hbm(gates))


def row_scale(route, expert, top_count):
    route = route.astype(jnp.float32)
    chosen = (route[:, :top_count] == expert.astype(jnp.float32)).astype(jnp.float32)
    weight = sum(route[:, top_count * part : top_count * (part + 1)] for part in (1, 2, 3))
    return jnp.sum(chosen * weight, axis=1, keepdims=True)


def expert_kernel(blocks, flips, with_prior, top_count, *refs):
    row_refs, refs = refs[:blocks], refs[blocks:]
    weight_refs, refs = refs[: 3 * len(flips)], refs[3 * len(flips) :]
    prior_refs, refs = (refs[:blocks], refs[blocks:]) if with_prior else ((), refs)
    out_refs, (rows_buf, total) = refs[:blocks], refs[blocks:]
    block_rows, width = out_refs[0].shape
    me = lax.axis_index("expert")
    for at in range(blocks):
        span = pl.ds(at * block_rows, block_rows)
        rows_buf[span, :] = row_refs[at][...]
        if with_prior:
            total[span, :] = prior_refs[at][...]
    rows = rows_buf[:, :width]
    for at, flip in enumerate(flips):
        gate_ref, up_ref, down_ref = weight_refs[3 * at : 3 * at + 3]
        scale = row_scale(rows_buf[:, width:], me ^ flip, top_count)
        gate_part = jnp.dot(rows, gate_ref[0], preferred_element_type=jnp.float32)
        up_part = jnp.dot(rows, up_ref[0], preferred_element_type=jnp.float32)
        hidden = (gate_part / (1.0 + jnp.exp(-gate_part)) * up_part).astype(jnp.bfloat16)
        result = jnp.dot(hidden, down_ref[0], preferred_element_type=jnp.float32) * scale
        if at or with_prior:
            total[...] += result
        else:
            total[...] = result
    for at in range(blocks):
        out_refs[at][...] = total[pl.ds(at * block_rows, block_rows), :]


def run_experts(made, top_count, row_blocks, flips, weights, prior=()):
    blocks, experts = len(row_blocks), len(weights)
    block_rows, row_width = row_blocks[0].shape
    _, width, hidden_width = weights[0][0].shape
    total = blocks * block_rows
    return pl.pallas_call(
        functools.partial(expert_kernel, blocks, flips, bool(prior), top_count),
        out_shape=[made((block_rows, width), jnp.float32)] * blocks,
        in_specs=[IN_VMEM] * (blocks + 3 * experts + len(prior)),
        out_specs=[IN_VMEM] * blocks,
        scratch_shapes=[
            pltpu.VMEM((total, row_width), jnp.bfloat16),
            pltpu.VMEM((total, width), jnp.float32),
        ],
        compiler_params=pltpu.CompilerParams(vmem_limit_bytes=SCOPED_BYTES),
        cost_estimate=pl.CostEstimate(
            flops=6 * total * width * hidden_width * experts,
            bytes_accessed=2 * (3 * width * hidden_width * experts + 2 * total * width),
            transcendentals=total * hidden_width * experts,
        ),
    )(
        *(made.pin(block) for block in row_blocks),
        *(made.pin(array) for weight in weights for array in weight),
        *(made.pin(block) for block in prior),
    )


def first_kernel(rows_ref, gate_in, up_in, hidden_ref, gate_ref, up_ref, parts, sems):
    width = gate_ref.shape[1]
    deep = even_split(width, DEPTH_STEP)
    sides = ((gate_in, gate_ref), (up_in, up_ref))

    def copies(at):
        span = pl.ds(at * deep, deep)
        return [
            pltpu.make_async_copy(source.at[0, span, :], kept.at[0, span, :], sems.at[side, at])
            for side, (source, kept) in enumerate(sides)
        ]

    steps = width // deep
    for at in range(steps):
        for copy in copies(at):
            copy.start()
    for at in range(steps):
        for copy in copies(at):
            copy.wait()
        span = pl.ds(at * deep, deep)
        for side, (_, kept) in enumerate(sides):
            now = jnp.dot(rows_ref[:, span], kept[0, span, :], preferred_element_type=jnp.float32)
            if at == 0:
                parts[side] = now
            else:
                parts[side] += now
    gate_part, up_part = parts[0], parts[1]
    hidden_ref[...] = (gate_part / (1.0 + jnp.exp(-gate_part)) * up_part).astype(jnp.bfloat16)


def second_kernel(top_count, rows_ref, hidden_ref, down_in, out_ref, down_ref, sems):
    hidden_width, width = down_ref.shape[1:]
    wide = even_split(hidden_width, HIDDEN_STEP)

    def copy(at):
        span = pl.ds(at * wide, wide)
        return pltpu.make_async_copy(down_in.at[0, span, :], down_ref.at[0, span, :], sems.at[at])

    steps = hidden_width // wide
    for at in range(steps):
        copy(at).start()
    scale = row_scale(rows_ref[:, width:], lax.axis_index("expert"), top_count)
    for at in range(steps):
        copy(at).wait()
        span = pl.ds(at * wide, wide)
        now = jnp.dot(hidden_ref[:, span], down_ref[0, span, :], preferred_element_type=jnp.float32)
        if at == 0:
            out_ref[...] = now
        else:
            out_ref[...] += now
    out_ref[...] = out_ref[...] * scale


def take_inputs_in(made, block, gate, up):
    _, width, hidden_width = gate.shape
    rows = block.shape[0]
    hidden, gate, up = pl.pallas_call(
        first_kernel,
        out_shape=[made((rows, hidden_width), jnp.bfloat16)] + [made(gate.shape, gate.dtype)] * 2,
        in_specs=[IN_VMEM] + [IN_HBM] * 2,
        out_specs=[IN_VMEM] * 3,
        scratch_shapes=[
            pltpu.VMEM((2, rows, hidden_width), jnp.float32),
            pltpu.SemaphoreType.DMA((2, width // even_split(width, DEPTH_STEP))),
        ],
        compiler_params=pltpu.CompilerParams(vmem_limit_bytes=SCOPED_BYTES),
        cost_estimate=pl.CostEstimate(
            flops=4 * rows * width * hidden_width,
            bytes_accessed=4 * width * hidden_width,
            transcendentals=rows * hidden_width,
        ),
    )(made.pin(block), in_hbm(gate), in_hbm(up))
    return hidden, gate, up


def take_output_in(made, top_count, block, hidden, down):
    _, hidden_width, width = down.shape
    rows = block.shape[0]
    return pl.pallas_call(
        functools.partial(second_kernel, top_count),
        out_shape=[made((rows, width), jnp.float32), made(down.shape, down.dtype)],
        in_specs=[IN_VMEM] * 2 + [IN_HBM],
        out_specs=[IN_VMEM] * 2,
        scratch_shapes=[
            pltpu.SemaphoreType.DMA((hidden_width // even_split(hidden_width, HIDDEN_STEP),))
        ],
        compiler_params=pltpu.CompilerParams(vmem_limit_bytes=SCOPED_BYTES),
        cost_estimate=pl.CostEstimate(
            flops=2 * rows * width * hidden_width,
            bytes_accessed=2 * width * hidden_width,
            transcendentals=0,
        ),
    )(made.pin(block), made.pin(hidden), in_hbm(down))


class InVmem:
    def __call__(self, shape, dtype):
        return pltpu.VMEM(shape, dtype)

    def pin(self, array):
        return pltpu.with_memory_space_constraint(array, pltpu.VMEM)


class Anywhere:
    def __call__(self, shape, dtype):
        return jax.ShapeDtypeStruct(shape, dtype)

    def pin(self, array):
        return array


def add_rounded(*terms):
    return sum(term.astype(jnp.float32) for term in terms).astype(jnp.bfloat16)


def shards(tokens, expert_ids, gate_weights, w_gate, w_up, w_down):
    local, width = tokens.shape
    top_count = expert_ids.shape[1]
    devices = lax.axis_size("expert")
    ring = chip_ring(devices // 2)
    ways = (ring_pairs(ring, 1), ring_pairs(ring, -1))
    siblings = [(at, at ^ 1) for at in range(devices)]
    hops = (len(ring) // 2, (len(ring) - 1) // 2)
    own = (w_gate, w_up, w_down)
    weight_bytes = 2 * sum(array.size * array.dtype.itemsize for array in own)
    kept_bytes = weight_bytes + len(ring) * local * width * 6
    made = InVmem() if kept_bytes <= KEPT_BYTES else Anywhere()
    run = functools.partial(run_experts, made, top_count)
    after = lax.optimization_barrier

    def outward(block, way):
        return lax.ppermute(block, "expert", ways[way])

    def homeward(block, way):
        return lax.ppermute(block, "expert", ways[1 - way])

    first = pack_rows(tokens, expert_ids, gate_weights, made)
    first, ready = after((first, own))
    other = tuple(lax.ppermute(array, "expert", siblings) for array in ready)

    rows = {(0, 0): first}
    partial = {}
    if hops[0]:
        rows[0, 1] = outward(first, 0)
    hidden, gate, up = take_inputs_in(made, first, w_gate, w_up)
    if hops[1]:
        later, hidden = after((first, hidden))
        rows[1, 1] = outward(later, 1)
    partial[0, 0], down = take_output_in(made, top_count, first, hidden, w_down)
    own = (gate, up, down)
    if hops[0]:
        rows[0, 1], partial[0, 0] = after((rows[0, 1], partial[0, 0]))
    for hop in range(2, hops[0] + 1):
        rows[0, hop] = outward(rows[0, hop - 1], 0)
        keys = [(0, hop - 1)] + [(1, hop - 2)] * (hop > 2)
        results = run([rows[key] for key in keys], (0,), [own])
        rows[1, hop - 1], results = after((rows[1, hop - 1], results))
        partial.update(zip(keys, results))
        if hop <= hops[1]:
            rows[1, hop] = outward(rows[1, hop - 1], 1)
    keys = [key for key in rows if key not in partial]
    if keys:
        results = run([rows[key] for key in keys], (0, 1), [own, other])
        partial.update(zip(keys, results))

    def sibling_sums(keys, prior):
        return run([rows[key] for key in keys], (1,), [other], prior)

    if hops[0] < 2:
        partial[0, 0] = sibling_sums([(0, 0)], [partial[0, 0]])[0]
    arrived = [None, None]
    level = list(hops)
    while level[0]:
        values = [None, None]
        values[0] = add_rounded(partial[0, level[0]], *[x for x in arrived[:1] if x is not None])
        arrived[0] = homeward(values[0], 0)
        keys = [(way, at - 1) for way, at in enumerate(level) if at > 1]
        keys = [key for key in keys if key in partial and key != (1, hops[0] - 1)]
        keys += [(0, 0)] * (level[0] == 2)
        waiting = arrived[1] if arrived[1] is not None else partial.get((1, level[1]))
        if keys:
            prior, _ = after(([partial[key] for key in keys], values[0]))
            waiting, results = after((waiting, sibling_sums(keys, prior)))
            partial.update(zip(keys, results))
        if level[1]:
            values[1] = add_rounded(*([waiting] if arrived[1] is None else [waiting, partial[1, level[1]]]))
            arrived[1] = homeward(values[1], 1)
        elif arrived[1] is not None:
            arrived[1] = waiting
        level = [max(at - 1, 0) for at in level]
    return add_rounded(partial[0, 0], *[value for value in arrived if value is not None])


def solution(mesh):
    placed = (
        P(("groups", "expert"), None),
        P(("groups", "expert"), None),
        P(("groups", "expert"), None),
        P("expert", None, None),
        P("expert", None, None),
        P("expert", None, None),
    )
    return jax.shard_map(
        shards, mesh=mesh, in_specs=placed, out_specs=P(("groups", "expert"), None), check_vma=False
    )
```

profile of v0, /device:TPU:17, one launch (start us, length us, event | category | flops | bytes accessed | tf_op | source)
XLA Modules:
  0.0 64.5 jit_solution(4078897553215053884)
XLA Ops:
  0.0 1.0 %shard_map.64.rows_ref.refs_1_ = bf16[64,2176]{1,0:T(8,128)(2,1)S(1)} custom-call(bf16[64,2048]{1,0:T(8,128)(2,1)} %tokens_ref.1, s32[8,64]{1,0:T(8,128)} %bitcast.2, f32[8,64]{1,0:T(8,128)} %bitcast.3), custom_call_target="tpu_custom_call" | custom-call | tf_op jit(solution)/shard_map/pallas_call | solution.py:85
  1.0 0.7 %collective-permute-start.7 = (bf16[1,2048,768]{2,1,0:T(8,128)(2,1)}, bf16[1,2048,768]{2,1,0:T(8,128)(2,1)S(1)}, u32[]{:S(2)}, u32[]{:S(2)}) collective-permute-start(bf16[1,2048,768]{2,1,0:T(8,128)(2,1)} %gate_in.1), channel_id=1, source_target_pairs={{0,1},{1,0},{2,3},{3,2},{4,5},{5,4},{6,7},{7,6},{8,9},{9,8},{10,11... | collective-permute-start | bytes 9437192 | tf_op jit(solution)/shard_map/ppermute | solution.py:299
  1.8 0.1 collective-permute-start.8
  1.8 0.4 collective-permute-start.9
  2.3 1.3 %collective-permute-start.1 = (bf16[64,2176]{1,0:T(8,128)(2,1)S(1)}, bf16[64,2176]{1,0:T(8,128)(2,1)S(1)}, u32[]{:S(2)}, u32[]{:S(2)}) collective-permute-start(bf16[64,2176]{1,0:T(8,128)(2,1)S(1)} %shard_map.64.rows_ref.refs_1_), channel_id=1, source_target_pairs={{0,3},{1,4},{2,1},{3,6},{6,11},{7,2},{10,7},{11,14},{14,13},{15,10... | collective-permute-start | bytes 835592 | tf_op jit(solution)/shard_map/ppermute | solution.py:292
  3.5 3.2 %shard_map.65 = (bf16[64,768]{1,0:T(8,128)(2,1)S(1)}, bf16[1,2048,768]{2,1,0:T(8,128)(2,1)S(1)}, bf16[1,2048,768]{2,1,0:T(8,128)(2,1)S(1)}) custom-call(bf16[64,2176]{1,0:T(8,128)(2,1)S(1)} %shard_map.64.rows_ref.refs_1_, bf16[1,2048,768]{2,1,0:T(8,128)(2,1)} %gate_in.1, bf16[1,2048,768]{2,1,0:T(8,128)(2,1)} %up_in.1), custom_call_target="tpu_custom_call" | custom-call | flops 402653184 | bytes 6291456 | tf_op jit(solution)/shard_map/pallas_call | solution.py:217
  6.8 0.5 collective-permute-start
  7.3 2.2 %shard_map.66 = (f32[64,2048]{1,0:T(8,128)S(1)}, bf16[1,768,2048]{2,1,0:T(8,128)(2,1)S(1)}) custom-call(bf16[64,2176]{1,0:T(8,128)(2,1)S(1)} %shard_map.64.rows_ref.refs_1_, bf16[64,768]{1,0:T(8,128)(2,1)S(1)} %get-tuple-element.56.hidden_ref, bf16[1,768,2048]{2,1,0:T(8,128)(2,1)} %down_in.1), custom_call_target="tpu_custom_call" | custom-call | flops 201326592 | bytes 3145728 | tf_op jit(solution)/shard_map/pallas_call | solution.py:239
  9.5 0.0 collective-permute-done.1.refs_0_
  9.5 1.3 %collective-permute-start.3 = (bf16[64,2176]{1,0:T(8,128)(2,1)S(1)}, bf16[64,2176]{1,0:T(8,128)(2,1)S(1)}, u32[]{:S(2)}, u32[]{:S(2)}) collective-permute-start(bf16[64,2176]{1,0:T(8,128)(2,1)S(1)} %collective-permute-done.1.refs_0_), channel_id=1, source_target_pairs={{0,3},{1,4},{2,1},{3,6},{6,11},{7,2},{10,7},{11,14},{14,13},{15,10... | collective-permute-start | bytes 835592 | tf_op jit(solution)/shard_map/ppermute | solution.py:292
  10.8 1.8 %shard_map.67.refs_5_ = f32[64,2048]{1,0:T(8,128)S(1)} custom-call(bf16[64,2176]{1,0:T(8,128)(2,1)S(1)} %collective-permute-done.1.refs_0_, bf16[1,2048,768]{2,1,0:T(8,128)(2,1)S(1)} %get-tuple-element.59.refs_1_.refs_2_, bf16[1,2048,768]{2,1,0:T(8,128)(2,1)S(1)} %get-tuple-element.60.refs_2_.refs_3_, bf16[1,768,2048]{2,1,0:T(8,128)(2,1)S(1)} %get-tuple-element.61.refs_3_.refs_4_), custom_call_target="tpu_custom_call" | custom-call | flops 603979776 | bytes 9961472 | tf_op jit(solution)/shard_map/pallas_call | solution.py:139
  12.6 1.3 %collective-permute-done.refs_1_ = bf16[64,2176]{1,0:T(8,128)(2,1)S(1)} collective-permute-done((bf16[64,2176]{1,0:T(8,128)(2,1)S(1)}, bf16[64,2176]{1,0:T(8,128)(2,1)S(1)}, u32[]{:S(2)}, u32[]{:S(2)}) %collective-permute-start) | collective-permute-done | bytes 278560 | tf_op jit(solution)/shard_map/ppermute | solution.py:292
  13.9 0.0 collective-permute-start.2
  13.9 3.0 %collective-permute-done.3.refs_0_ = bf16[64,2176]{1,0:T(8,128)(2,1)S(1)} collective-permute-done((bf16[64,2176]{1,0:T(8,128)(2,1)S(1)}, bf16[64,2176]{1,0:T(8,128)(2,1)S(1)}, u32[]{:S(2)}, u32[]{:S(2)}) %collective-permute-start.3) | collective-permute-done | bytes 278560 | tf_op jit(solution)/shard_map/ppermute | solution.py:292
  16.9 0.5 collective-permute-start.5
  17.4 1.5 %shard_map.68 = (f32[64,2048]{1,0:T(8,128)S(1)}, f32[64,2048]{1,0:T(8,128)S(1)}) custom-call(bf16[64,2176]{1,0:T(8,128)(2,1)S(1)} %collective-permute-done.3.refs_0_, bf16[64,2176]{1,0:T(8,128)(2,1)S(1)} %collective-permute-done.refs_1_, bf16[1,2048,768]{2,1,0:T(8,128)(2,1)S(1)} %get-tuple-element.59.refs_1_.refs_2_, ...), custom_call_target="tpu_custom_call" | custom-call | flops 1207959552 | bytes 10485760 | tf_op jit(solution)/shard_map/pallas_call | solution.py:139
  18.9 2.3 %collective-permute-done.2.refs_1_ = bf16[64,2176]{1,0:T(8,128)(2,1)S(1)} collective-permute-done((bf16[64,2176]{1,0:T(8,128)(2,1)S(1)}, bf16[64,2176]{1,0:T(8,128)(2,1)S(1)}, u32[]{:S(2)}, u32[]{:S(2)}) %collective-permute-start.2) | collective-permute-done | bytes 278560 | tf_op jit(solution)/shard_map/ppermute | solution.py:292
  21.2 0.0 collective-permute-start.4
  21.2 3.3 %collective-permute-done.5.refs_0_ = bf16[64,2176]{1,0:T(8,128)(2,1)S(1)} collective-permute-done((bf16[64,2176]{1,0:T(8,128)(2,1)S(1)}, bf16[64,2176]{1,0:T(8,128)(2,1)S(1)}, u32[]{:S(2)}, u32[]{:S(2)}) %collective-permute-start.5) | collective-permute-done | bytes 278560 | tf_op jit(solution)/shard_map/ppermute | solution.py:292
  24.5 0.3 collective-permute-start.6
  24.7 1.5 %shard_map.69 = (f32[64,2048]{1,0:T(8,128)S(1)}, f32[64,2048]{1,0:T(8,128)S(1)}) custom-call(bf16[64,2176]{1,0:T(8,128)(2,1)S(1)} %collective-permute-done.5.refs_0_, bf16[64,2176]{1,0:T(8,128)(2,1)S(1)} %collective-permute-done.2.refs_1_, bf16[1,2048,768]{2,1,0:T(8,128)(2,1)S(1)} %get-tuple-element.59.refs_1_.refs_2_, ...), custom_call_target="tpu_custom_call" | custom-call | flops 1207959552 | bytes 10485760 | tf_op jit(solution)/shard_map/pallas_call | solution.py:139
  26.2 2.4 %collective-permute-done.4.refs_0_ = bf16[64,2176]{1,0:T(8,128)(2,1)S(1)} collective-permute-done((bf16[64,2176]{1,0:T(8,128)(2,1)S(1)}, bf16[64,2176]{1,0:T(8,128)(2,1)S(1)}, u32[]{:S(2)}, u32[]{:S(2)}) %collective-permute-start.4) | collective-permute-done | bytes 278560 | tf_op jit(solution)/shard_map/ppermute | solution.py:292
  28.7 1.8 %collective-permute-done.6.refs_1_ = bf16[64,2176]{1,0:T(8,128)(2,1)S(1)} collective-permute-done((bf16[64,2176]{1,0:T(8,128)(2,1)S(1)}, bf16[64,2176]{1,0:T(8,128)(2,1)S(1)}, u32[]{:S(2)}, u32[]{:S(2)}) %collective-permute-start.6) | collective-permute-done | bytes 278560 | tf_op jit(solution)/shard_map/ppermute | solution.py:292
  30.4 0.0 collective-permute-done.7.refs_5_.refs_2_
  30.5 0.0 collective-permute-done.8.refs_6_.refs_3_
  30.5 0.0 collective-permute-done.9.refs_7_.refs_4_
  30.5 2.8 %shard_map.70 = (f32[64,2048]{1,0:T(8,128)S(1)}, f32[64,2048]{1,0:T(8,128)S(1)}) custom-call(bf16[64,2176]{1,0:T(8,128)(2,1)S(1)} %collective-permute-done.4.refs_0_, bf16[64,2176]{1,0:T(8,128)(2,1)S(1)} %collective-permute-done.6.refs_1_, bf16[1,2048,768]{2,1,0:T(8,128)(2,1)S(1)} %get-tuple-element.59.refs_1_.refs_2_, ...), custom_call_target="tpu_custom_call" | custom-call | flops 2415919104 | bytes 19922944 | tf_op jit(solution)/shard_map/pallas_call | solution.py:139
  33.3 0.1 collective-permute-start.11
  33.4 1.5 %shard_map.71 = (f32[64,2048]{1,0:T(8,128)S(1)}, f32[64,2048]{1,0:T(8,128)S(1)}) custom-call(bf16[64,2176]{1,0:T(8,128)(2,1)S(1)} %collective-permute-done.5.refs_0_, bf16[64,2176]{1,0:T(8,128)(2,1)S(1)} %collective-permute-done.2.refs_1_, bf16[1,2048,768]{2,1,0:T(8,128)(2,1)S(1)} %collective-permute-done.7.refs_5_.refs_2_, ...), custom_call_target="tpu_custom_call" | custom-call | flops 1207959552 | bytes 10485760 | tf_op jit(solution)/shard_map/pallas_call | solution.py:139
  34.9 1.8 %collective-permute-start.10 = (bf16[64,2048]{1,0:T(8,128)(2,1)S(1)}, bf16[64,2048]{1,0:T(8,128)(2,1)S(1)}, u32[]{:S(2)}, u32[]{:S(2)}) collective-permute-start(bf16[64,2048]{1,0:T(8,128)(2,1)S(1)} %convert_element_type.46), channel_id=1, source_target_pairs={{0,3},{1,4},{2,1},{3,6},{6,11},{7,2},{10,7},{11,14},{14,13},{15,10... | collective-permute-start | bytes 786440 | tf_op jit(solution)/shard_map/ppermute | solution.py:295
  36.7 4.3 %collective-permute-done.11 = bf16[64,2048]{1,0:T(8,128)(2,1)S(1)} collective-permute-done((bf16[64,2048]{1,0:T(8,128)(2,1)S(1)}, bf16[64,2048]{1,0:T(8,128)(2,1)S(1)}, u32[]{:S(2)}, u32[]{:S(2)}) %collective-permute-start.11) | collective-permute-done | bytes 262176 | tf_op jit(solution)/shard_map/ppermute | solution.py:295
  41.0 0.2 collective-permute-start.13
  41.2 1.5 %shard_map.72 = (f32[64,2048]{1,0:T(8,128)S(1)}, f32[64,2048]{1,0:T(8,128)S(1)}) custom-call(bf16[64,2176]{1,0:T(8,128)(2,1)S(1)} %collective-permute-done.3.refs_0_, bf16[64,2176]{1,0:T(8,128)(2,1)S(1)} %collective-permute-done.refs_1_, bf16[1,2048,768]{2,1,0:T(8,128)(2,1)S(1)} %collective-permute-done.7.refs_5_.refs_2_, ...), custom_call_target="tpu_custom_call" | custom-call | flops 1207959552 | bytes 10485760 | tf_op jit(solution)/shard_map/pallas_call | solution.py:139
  42.7 0.0 collective-permute-done.10
  42.7 0.1 add_convert_fusion.4
  42.8 1.8 %collective-permute-start.12 = (bf16[64,2048]{1,0:T(8,128)(2,1)S(1)}, bf16[64,2048]{1,0:T(8,128)(2,1)S(1)}, u32[]{:S(2)}, u32[]{:S(2)}) collective-permute-start(bf16[64,2048]{1,0:T(8,128)(2,1)S(1)} %add_convert_fusion.4), channel_id=1, source_target_pairs={{0,3},{1,4},{2,1},{3,6},{6,11},{7,2},{10,7},{11,14},{14,13},{15,10... | collective-permute-start | bytes 786440 | tf_op jit(solution)/shard_map/ppermute | solution.py:295
  44.6 4.7 %collective-permute-done.13 = bf16[64,2048]{1,0:T(8,128)(2,1)S(1)} collective-permute-done((bf16[64,2048]{1,0:T(8,128)(2,1)S(1)}, bf16[64,2048]{1,0:T(8,128)(2,1)S(1)}, u32[]{:S(2)}, u32[]{:S(2)}) %collective-permute-start.13) | collective-permute-done | bytes 262176 | tf_op jit(solution)/shard_map/ppermute | solution.py:295
  49.4 0.1 collective-permute-start.14
  49.4 1.5 %shard_map.73 = (f32[64,2048]{1,0:T(8,128)S(1)}, f32[64,2048]{1,0:T(8,128)S(1)}) custom-call(bf16[64,2176]{1,0:T(8,128)(2,1)S(1)} %collective-permute-done.1.refs_0_, bf16[64,2176]{1,0:T(8,128)(2,1)S(1)} %shard_map.64.rows_ref.refs_1_, bf16[1,2048,768]{2,1,0:T(8,128)(2,1)S(1)} %collective-permute-done.7.refs_5_.refs_2_, ...), custom_call_target="tpu_custom_call" | custom-call | flops 1207959552 | bytes 10485760 | tf_op jit(solution)/shard_map/pallas_call | solution.py:139
  50.9 0.0 collective-permute-done.12
  50.9 0.1 add_convert_fusion.1
  51.0 1.8 %collective-permute-start.16 = (bf16[64,2048]{1,0:T(8,128)(2,1)S(1)}, bf16[64,2048]{1,0:T(8,128)(2,1)S(1)}, u32[]{:S(2)}, u32[]{:S(2)}) collective-permute-start(bf16[64,2048]{1,0:T(8,128)(2,1)S(1)} %add_convert_fusion.1), channel_id=1, source_target_pairs={{0,3},{1,4},{2,1},{3,6},{6,11},{7,2},{10,7},{11,14},{14,13},{15,10... | collective-permute-start | bytes 786440 | tf_op jit(solution)/shard_map/ppermute | solution.py:295
  52.8 5.1 %collective-permute-done.14 = bf16[64,2048]{1,0:T(8,128)(2,1)S(1)} collective-permute-done((bf16[64,2048]{1,0:T(8,128)(2,1)S(1)}, bf16[64,2048]{1,0:T(8,128)(2,1)S(1)}, u32[]{:S(2)}, u32[]{:S(2)}) %collective-permute-start.14) | collective-permute-done | bytes 262176 | tf_op jit(solution)/shard_map/ppermute | solution.py:295
  57.9 0.1 collective-permute-start.15
  57.9 0.7 %collective-permute-done.16 = bf16[64,2048]{1,0:T(8,128)(2,1)S(1)} collective-permute-done((bf16[64,2048]{1,0:T(8,128)(2,1)S(1)}, bf16[64,2048]{1,0:T(8,128)(2,1)S(1)}, u32[]{:S(2)}, u32[]{:S(2)}) %collective-permute-start.16) | collective-permute-done | bytes 262176 | tf_op jit(solution)/shard_map/ppermute | solution.py:295
  58.7 5.1 %collective-permute-done.15 = bf16[64,2048]{1,0:T(8,128)(2,1)S(1)} collective-permute-done((bf16[64,2048]{1,0:T(8,128)(2,1)S(1)}, bf16[64,2048]{1,0:T(8,128)(2,1)S(1)}, u32[]{:S(2)}, u32[]{:S(2)}) %collective-permute-start.15) | collective-permute-done | bytes 262176 | tf_op jit(solution)/shard_map/ppermute | solution.py:295
  63.7 0.8 %add_convert_fusion = bf16[64,2048]{1,0:T(8,128)(2,1)} fusion(bf16[64,2048]{1,0:T(8,128)(2,1)S(1)} %collective-permute-done.16, f32[64,2048]{1,0:T(8,128)S(1)} %get-tuple-element.97, bf16[64,2048]{1,0:T(8,128)(2,1)S(1)} %collective-permute-done.15), kind=kLoop, calls=%fused_computation | loop fusion | flops 655360 | bytes 1310720 | tf_op jit(solution)/shard_map/convert_element_type | solution.py:273
  (5 shorter events, 0.2 us)
Async XLA Ops:
  1.0 29.4 %collective-permute-start.7 = (bf16[1,2048,768]{2,1,0:T(8,128)(2,1)}, bf16[1,2048,768]{2,1,0:T(8,128)(2,1)S(1)}, u32[]{:S(2)}, u32[]{:S(2)}) collective-permute-start(bf16[1,2048,768]{2,1,0:T(8,128)(2,1)} %gate_in.1), channel_id=1, source_target_pairs={{0,1},{1,0},{2,3},{3,2},{4,5},{5,4},{6,7},{7,6},{8,9},{9,8},{10,11... | collective-permute-start | bytes 9437192 | tf_op jit(solution)/shard_map/ppermute | solution.py:299
  1.8 28.7 %collective-permute-start.8 = (bf16[1,2048,768]{2,1,0:T(8,128)(2,1)}, bf16[1,2048,768]{2,1,0:T(8,128)(2,1)S(1)}, u32[]{:S(2)}, u32[]{:S(2)}) collective-permute-start(bf16[1,2048,768]{2,1,0:T(8,128)(2,1)} %up_in.1), channel_id=1, source_target_pairs={{0,1},{1,0},{2,3},{3,2},{4,5},{5,4},{6,7},{7,6},{8,9},{9,8},{10,11... | collective-permute-start | bytes 9437192 | tf_op jit(solution)/shard_map/ppermute | solution.py:299
  1.8 28.6 %collective-permute-start.9 = (bf16[1,768,2048]{2,1,0:T(8,128)(2,1)}, bf16[1,768,2048]{2,1,0:T(8,128)(2,1)S(1)}, u32[]{:S(2)}, u32[]{:S(2)}) collective-permute-start(bf16[1,768,2048]{2,1,0:T(8,128)(2,1)} %down_in.1), channel_id=1, source_target_pairs={{0,1},{1,0},{2,3},{3,2},{4,5},{5,4},{6,7},{7,6},{8,9},{9,8},{10,11... | collective-permute-start | bytes 9437192 | tf_op jit(solution)/shard_map/ppermute | solution.py:299
  2.3 7.2 %collective-permute-start.1 = (bf16[64,2176]{1,0:T(8,128)(2,1)S(1)}, bf16[64,2176]{1,0:T(8,128)(2,1)S(1)}, u32[]{:S(2)}, u32[]{:S(2)}) collective-permute-start(bf16[64,2176]{1,0:T(8,128)(2,1)S(1)} %shard_map.64.rows_ref.refs_1_), channel_id=1, source_target_pairs={{0,3},{1,4},{2,1},{3,6},{6,11},{7,2},{10,7},{11,14},{14,13},{15,10... | collective-permute-start | bytes 835592 | tf_op jit(solution)/shard_map/ppermute | solution.py:292
  6.8 7.1 %collective-permute-start = (bf16[64,2176]{1,0:T(8,128)(2,1)S(1)}, bf16[64,2176]{1,0:T(8,128)(2,1)S(1)}, u32[]{:S(2)}, u32[]{:S(2)}) collective-permute-start(bf16[64,2176]{1,0:T(8,128)(2,1)S(1)} %shard_map.64.rows_ref.refs_1_), channel_id=1, source_target_pairs={{0,5},{1,2},{2,7},{3,0},{6,3},{7,10},{10,15},{11,6},{14,11},{15,12... | collective-permute-start | bytes 835592 | tf_op jit(solution)/shard_map/ppermute | solution.py:292
  9.5 7.4 %collective-permute-start.3 = (bf16[64,2176]{1,0:T(8,128)(2,1)S(1)}, bf16[64,2176]{1,0:T(8,128)(2,1)S(1)}, u32[]{:S(2)}, u32[]{:S(2)}) collective-permute-start(bf16[64,2176]{1,0:T(8,128)(2,1)S(1)} %collective-permute-done.1.refs_0_), channel_id=1, source_target_pairs={{0,3},{1,4},{2,1},{3,6},{6,11},{7,2},{10,7},{11,14},{14,13},{15,10... | collective-permute-start | bytes 835592 | tf_op jit(solution)/shard_map/ppermute | solution.py:292
  13.9 7.3 %collective-permute-start.2 = (bf16[64,2176]{1,0:T(8,128)(2,1)S(1)}, bf16[64,2176]{1,0:T(8,128)(2,1)S(1)}, u32[]{:S(2)}, u32[]{:S(2)}) collective-permute-start(bf16[64,2176]{1,0:T(8,128)(2,1)S(1)} %collective-permute-done.refs_1_), channel_id=1, source_target_pairs={{0,5},{1,2},{2,7},{3,0},{6,3},{7,10},{10,15},{11,6},{14,11},{15,12... | collective-permute-start | bytes 835592 | tf_op jit(solution)/shard_map/ppermute | solution.py:292
  16.9 7.6 %collective-permute-start.5 = (bf16[64,2176]{1,0:T(8,128)(2,1)S(1)}, bf16[64,2176]{1,0:T(8,128)(2,1)S(1)}, u32[]{:S(2)}, u32[]{:S(2)}) collective-permute-start(bf16[64,2176]{1,0:T(8,128)(2,1)S(1)} %collective-permute-done.3.refs_0_), channel_id=1, source_target_pairs={{0,3},{1,4},{2,1},{3,6},{6,11},{7,2},{10,7},{11,14},{14,13},{15,10... | collective-permute-start | bytes 835592 | tf_op jit(solution)/shard_map/ppermute | solution.py:292
  21.2 7.5 %collective-permute-start.4 = (bf16[64,2176]{1,0:T(8,128)(2,1)S(1)}, bf16[64,2176]{1,0:T(8,128)(2,1)S(1)}, u32[]{:S(2)}, u32[]{:S(2)}) collective-permute-start(bf16[64,2176]{1,0:T(8,128)(2,1)S(1)} %collective-permute-done.2.refs_1_), channel_id=1, source_target_pairs={{0,5},{1,2},{2,7},{3,0},{6,3},{7,10},{10,15},{11,6},{14,11},{15,12... | collective-permute-start | bytes 835592 | tf_op jit(solution)/shard_map/ppermute | solution.py:292
  24.5 6.0 %collective-permute-start.6 = (bf16[64,2176]{1,0:T(8,128)(2,1)S(1)}, bf16[64,2176]{1,0:T(8,128)(2,1)S(1)}, u32[]{:S(2)}, u32[]{:S(2)}) collective-permute-start(bf16[64,2176]{1,0:T(8,128)(2,1)S(1)} %collective-permute-done.5.refs_0_), channel_id=1, source_target_pairs={{0,3},{1,4},{2,1},{3,6},{6,11},{7,2},{10,7},{11,14},{14,13},{15,10... | collective-permute-start | bytes 835592 | tf_op jit(solution)/shard_map/ppermute | solution.py:292
  33.3 7.6 %collective-permute-start.11 = (bf16[64,2048]{1,0:T(8,128)(2,1)S(1)}, bf16[64,2048]{1,0:T(8,128)(2,1)S(1)}, u32[]{:S(2)}, u32[]{:S(2)}) collective-permute-start(bf16[64,2048]{1,0:T(8,128)(2,1)S(1)} %convert_element_type.45), channel_id=1, source_target_pairs={{0,5},{1,2},{2,7},{3,0},{6,3},{7,10},{10,15},{11,6},{14,11},{15,12... | collective-permute-start | bytes 786440 | tf_op jit(solution)/shard_map/ppermute | solution.py:295
  34.9 7.8 %collective-permute-start.10 = (bf16[64,2048]{1,0:T(8,128)(2,1)S(1)}, bf16[64,2048]{1,0:T(8,128)(2,1)S(1)}, u32[]{:S(2)}, u32[]{:S(2)}) collective-permute-start(bf16[64,2048]{1,0:T(8,128)(2,1)S(1)} %convert_element_type.46), channel_id=1, source_target_pairs={{0,3},{1,4},{2,1},{3,6},{6,11},{7,2},{10,7},{11,14},{14,13},{15,10... | collective-permute-start | bytes 786440 | tf_op jit(solution)/shard_map/ppermute | solution.py:295
  41.0 8.3 %collective-permute-start.13 = (bf16[64,2048]{1,0:T(8,128)(2,1)S(1)}, bf16[64,2048]{1,0:T(8,128)(2,1)S(1)}, u32[]{:S(2)}, u32[]{:S(2)}) collective-permute-start(bf16[64,2048]{1,0:T(8,128)(2,1)S(1)} %add_convert_fusion.5), channel_id=1, source_target_pairs={{0,5},{1,2},{2,7},{3,0},{6,3},{7,10},{10,15},{11,6},{14,11},{15,12... | collective-permute-start | bytes 786440 | tf_op jit(solution)/shard_map/ppermute | solution.py:295
  42.8 8.1 %collective-permute-start.12 = (bf16[64,2048]{1,0:T(8,128)(2,1)S(1)}, bf16[64,2048]{1,0:T(8,128)(2,1)S(1)}, u32[]{:S(2)}, u32[]{:S(2)}) collective-permute-start(bf16[64,2048]{1,0:T(8,128)(2,1)S(1)} %add_convert_fusion.4), channel_id=1, source_target_pairs={{0,3},{1,4},{2,1},{3,6},{6,11},{7,2},{10,7},{11,14},{14,13},{15,10... | collective-permute-start | bytes 786440 | tf_op jit(solution)/shard_map/ppermute | solution.py:295
  49.4 8.5 %collective-permute-start.14 = (bf16[64,2048]{1,0:T(8,128)(2,1)S(1)}, bf16[64,2048]{1,0:T(8,128)(2,1)S(1)}, u32[]{:S(2)}, u32[]{:S(2)}) collective-permute-start(bf16[64,2048]{1,0:T(8,128)(2,1)S(1)} %add_convert_fusion.3), channel_id=1, source_target_pairs={{0,5},{1,2},{2,7},{3,0},{6,3},{7,10},{10,15},{11,6},{14,11},{15,12... | collective-permute-start | bytes 786440 | tf_op jit(solution)/shard_map/ppermute | solution.py:295
  51.0 7.7 %collective-permute-start.16 = (bf16[64,2048]{1,0:T(8,128)(2,1)S(1)}, bf16[64,2048]{1,0:T(8,128)(2,1)S(1)}, u32[]{:S(2)}, u32[]{:S(2)}) collective-permute-start(bf16[64,2048]{1,0:T(8,128)(2,1)S(1)} %add_convert_fusion.1), channel_id=1, source_target_pairs={{0,3},{1,4},{2,1},{3,6},{6,11},{7,2},{10,7},{11,14},{14,13},{15,10... | collective-permute-start | bytes 786440 | tf_op jit(solution)/shard_map/ppermute | solution.py:295
  57.9 5.8 %collective-permute-start.15 = (bf16[64,2048]{1,0:T(8,128)(2,1)S(1)}, bf16[64,2048]{1,0:T(8,128)(2,1)S(1)}, u32[]{:S(2)}, u32[]{:S(2)}) collective-permute-start(bf16[64,2048]{1,0:T(8,128)(2,1)S(1)} %add_convert_fusion.2), channel_id=1, source_target_pairs={{0,5},{1,2},{2,7},{3,0},{6,3},{7,10},{10,15},{11,6},{14,11},{15,12... | collective-permute-start | bytes 786440 | tf_op jit(solution)/shard_map/ppermute | solution.py:295
where the time goes:
time: 64.7 us; the launch traced here: 64.5 us
  waiting for transfers between devices  33.9 us (52%)
  Pallas kernels  18.4 us (28%)
  starting transfers between devices  10.9 us (17%)
  other arithmetic  1.13 us (2%)
    ppermute x7, waiting for transfers between devices, homeward(): return lax.ppermute(block, 'expert', ways[1 - way])  19.8 us
    ppermute x7, waiting for transfers between devices, outward(): return lax.ppermute(block, 'expert', ways[way])  14.1 us
    pallas_call x7, Pallas kernels, run_experts(): pl.pallas_call(functools.partial(expert_kernel, blocks, flips, bool(prior...  12 us
    ppermute x7, starting transfers between devices, homeward(): return lax.ppermute(block, 'expert', ways[1 - way])  5.76 us
    ppermute x7, starting transfers between devices, outward(): return lax.ppermute(block, 'expert', ways[way])  3.85 us
    pallas_call x1, Pallas kernels, take_inputs_in(): pl.pallas_call(first_kernel, out_shape=[made((rows, hidden_width), jnp.bf...  3.25 us
    pallas_call x1, Pallas kernels, take_output_in(): pl.pallas_call(functools.partial(second_kernel, top_count), out_shape=[ma...  2.18 us
  transfers between devices with their start and end apart: 17, of which 11 were waited for; matrix products, arithmetic and copies ran while one was open for 0% of the time, Pallas kernels for 23%

commit v1 on v0

--- a/solution.py
+++ b/solution.py
@@ -313,7 +313,7 @@
     for hop in range(2, hops[0] + 1):
         rows[0, hop] = outward(rows[0, hop - 1], 0)
         keys = [(0, hop - 1)] + [(1, hop - 2)] * (hop > 2)
-        results = run([rows[key] for key in keys], (0,), [own])
+        results = [run([rows[key]], (0,), [own])[0] for key in keys]
         rows[1, hop - 1], results = after((rows[1, hop - 1], results))
         partial.update(zip(keys, results))
         if hop <= hops[1]:
@@ -324,7 +324,7 @@
         partial.update(zip(keys, results))
 
     def sibling_sums(keys, prior):
-        return run([rows[key] for key in keys], (1,), [other], prior)
+        return [run([rows[key]], (1,), [other], [value])[0] for key, value in zip(keys, prior)]
 
     if hops[0] < 2:
         partial[0, 0] = sibling_sums([(0, 0)], [partial[0, 0]])[0]

time: 64.7 us -> 67.5 us (1.043)
  the two profiles are of different devices: /device:TPU:17 before, /device:TPU:0 now
where the time goes in v1:
time: 67.5 us; the launch traced here: 67.3 us
  Pallas kernels  29.1 us (43%)
  waiting for transfers between devices  24.4 us (36%)
  starting transfers between devices  12.4 us (18%)
  other arithmetic  1.14 us (2%)
    pallas_call x12, Pallas kernels, run_experts(): pl.pallas_call(functools.partial(expert_kernel, blocks, flips, bool(prior...  22.7 us
    ppermute x7, waiting for transfers between devices, homeward(): return lax.ppermute(block, 'expert', ways[1 - way])  15.5 us
    ppermute x7, waiting for transfers between devices, outward(): return lax.ppermute(block, 'expert', ways[way])  8.93 us
    ppermute x7, starting transfers between devices, outward(): return lax.ppermute(block, 'expert', ways[way])  6.66 us
    ppermute x7, starting transfers between devices, homeward(): return lax.ppermute(block, 'expert', ways[1 - way])  4.76 us
    pallas_call x1, Pallas kernels, take_inputs_in(): pl.pallas_call(first_kernel, out_shape=[made((rows, hidden_width), jnp.bf...  3.25 us
    pallas_call x1, Pallas kernels, take_output_in(): pl.pallas_call(functools.partial(second_kernel, top_count), out_shape=[ma...  2.18 us
  transfers between devices with their start and end apart: 17, of which 12 were waited for; matrix products, arithmetic and copies ran while one was open for 0% of the time, Pallas kernels for 38%

profile of v1, /device:TPU:0, one launch (start us, length us, event | category | flops | bytes accessed | tf_op | source)
XLA Modules:
  0.0 67.3 jit_solution(10759995417335947030)
XLA Ops:
  0.0 1.0 %shard_map.64.rows_ref.refs_0_ = bf16[64,2176]{1,0:T(8,128)(2,1)S(1)} custom-call(bf16[64,2048]{1,0:T(8,128)(2,1)} %tokens_ref.1, s32[8,64]{1,0:T(8,128)} %bitcast.2, f32[8,64]{1,0:T(8,128)} %bitcast.3), custom_call_target="tpu_custom_call" | custom-call | tf_op jit(solution)/shard_map/pallas_call | solution.py:85
  1.0 0.5 collective-permute-start.7
  1.5 0.1 collective-permute-start.8
  1.6 0.4 collective-permute-start.9
  2.0 2.6 %collective-permute-start.1 = (bf16[64,2176]{1,0:T(8,128)(2,1)S(1)}, bf16[64,2176]{1,0:T(8,128)(2,1)S(1)}, u32[]{:S(2)}, u32[]{:S(2)}) collective-permute-start(bf16[64,2176]{1,0:T(8,128)(2,1)S(1)} %shard_map.64.rows_ref.refs_0_), channel_id=1, source_target_pairs={{0,3},{1,4},{2,1},{3,6},{6,11},{7,2},{10,7},{11,14},{14,13},{15,10... | collective-permute-start | bytes 835592 | tf_op jit(solution)/shard_map/ppermute | solution.py:292
  4.7 3.2 %shard_map.65 = (bf16[64,768]{1,0:T(8,128)(2,1)S(1)}, bf16[1,2048,768]{2,1,0:T(8,128)(2,1)S(1)}, bf16[1,2048,768]{2,1,0:T(8,128)(2,1)S(1)}) custom-call(bf16[64,2176]{1,0:T(8,128)(2,1)S(1)} %shard_map.64.rows_ref.refs_0_, bf16[1,2048,768]{2,1,0:T(8,128)(2,1)} %gate_in.1, bf16[1,2048,768]{2,1,0:T(8,128)(2,1)} %up_in.1), custom_call_target="tpu_custom_call" | custom-call | flops 402653184 | bytes 6291456 | tf_op jit(solution)/shard_map/pallas_call | solution.py:217
  7.9 0.1 collective-permute-start
  8.0 2.2 %shard_map.66 = (f32[64,2048]{1,0:T(8,128)S(1)}, bf16[1,768,2048]{2,1,0:T(8,128)(2,1)S(1)}) custom-call(bf16[64,2176]{1,0:T(8,128)(2,1)S(1)} %shard_map.64.rows_ref.refs_0_, bf16[64,768]{1,0:T(8,128)(2,1)S(1)} %get-tuple-element.46.hidden_ref, bf16[1,768,2048]{2,1,0:T(8,128)(2,1)} %down_in.1), custom_call_target="tpu_custom_call" | custom-call | flops 201326592 | bytes 3145728 | tf_op jit(solution)/shard_map/pallas_call | solution.py:239
  10.2 0.0 collective-permute-done.1.refs_0_
  10.2 1.7 %collective-permute-start.3 = (bf16[64,2176]{1,0:T(8,128)(2,1)S(1)}, bf16[64,2176]{1,0:T(8,128)(2,1)S(1)}, u32[]{:S(2)}, u32[]{:S(2)}) collective-permute-start(bf16[64,2176]{1,0:T(8,128)(2,1)S(1)} %collective-permute-done.1.refs_0_), channel_id=1, source_target_pairs={{0,3},{1,4},{2,1},{3,6},{6,11},{7,2},{10,7},{11,14},{14,13},{15,10... | collective-permute-start | bytes 835592 | tf_op jit(solution)/shard_map/ppermute | solution.py:292
  12.0 1.8 %shard_map.67.refs_4_ = f32[64,2048]{1,0:T(8,128)S(1)} custom-call(bf16[64,2176]{1,0:T(8,128)(2,1)S(1)} %collective-permute-done.1.refs_0_, bf16[1,2048,768]{2,1,0:T(8,128)(2,1)S(1)} %get-tuple-element.49.refs_1_.refs_2_, bf16[1,2048,768]{2,1,0:T(8,128)(2,1)S(1)} %get-tuple-element.50.refs_2_.refs_3_, bf16[1,768,2048]{2,1,0:T(8,128)(2,1)S(1)} %get-tuple-element.51.refs_3_.refs_4_), custom_call_target="tpu_custom_call" | custom-call | flops 603979776 | bytes 9961472 | tf_op jit(solution)/shard_map/pallas_call | solution.py:139
  13.8 0.5 collective-permute-done.refs_0_
  14.3 0.0 collective-permute-start.2
  14.3 2.9 %collective-permute-done.3.refs_0_ = bf16[64,2176]{1,0:T(8,128)(2,1)S(1)} collective-permute-done((bf16[64,2176]{1,0:T(8,128)(2,1)S(1)}, bf16[64,2176]{1,0:T(8,128)(2,1)S(1)}, u32[]{:S(2)}, u32[]{:S(2)}) %collective-permute-start.3) | collective-permute-done | bytes 278560 | tf_op jit(solution)/shard_map/ppermute | solution.py:292
  17.3 1.3 %collective-permute-start.5 = (bf16[64,2176]{1,0:T(8,128)(2,1)S(1)}, bf16[64,2176]{1,0:T(8,128)(2,1)S(1)}, u32[]{:S(2)}, u32[]{:S(2)}) collective-permute-start(bf16[64,2176]{1,0:T(8,128)(2,1)S(1)} %collective-permute-done.3.refs_0_), channel_id=1, source_target_pairs={{0,3},{1,4},{2,1},{3,6},{6,11},{7,2},{10,7},{11,14},{14,13},{15,10... | collective-permute-start | bytes 835592 | tf_op jit(solution)/shard_map/ppermute | solution.py:292
  18.5 1.8 %shard_map.69.refs_4_ = f32[64,2048]{1,0:T(8,128)S(1)} custom-call(bf16[64,2176]{1,0:T(8,128)(2,1)S(1)} %collective-permute-done.refs_0_, bf16[1,2048,768]{2,1,0:T(8,128)(2,1)S(1)} %get-tuple-element.49.refs_1_.refs_2_, bf16[1,2048,768]{2,1,0:T(8,128)(2,1)S(1)} %get-tuple-element.50.refs_2_.refs_3_, bf16[1,768,2048]{2,1,0:T(8,128)(2,1)S(1)} %get-tuple-element.51.refs_3_.refs_4_), custom_call_target="tpu_custom_call" | custom-call | flops 603979776 | bytes 9961472 | tf_op jit(solution)/shard_map/pallas_call | solution.py:139
  20.3 1.8 %shard_map.68.refs_4_ = f32[64,2048]{1,0:T(8,128)S(1)} custom-call(bf16[64,2176]{1,0:T(8,128)(2,1)S(1)} %collective-permute-done.3.refs_0_, bf16[1,2048,768]{2,1,0:T(8,128)(2,1)S(1)} %get-tuple-element.49.refs_1_.refs_2_, bf16[1,2048,768]{2,1,0:T(8,128)(2,1)S(1)} %get-tuple-element.50.refs_2_.refs_3_, bf16[1,768,2048]{2,1,0:T(8,128)(2,1)S(1)} %get-tuple-element.51.refs_3_.refs_4_), custom_call_target="tpu_custom_call" | custom-call | flops 603979776 | bytes 9961472 | tf_op jit(solution)/shard_map/pallas_call | solution.py:139
  22.2 0.0 collective-permute-done.2.refs_0_
  22.2 0.5 collective-permute-start.4
  22.7 1.8 %collective-permute-done.5.refs_0_ = bf16[64,2176]{1,0:T(8,128)(2,1)S(1)} collective-permute-done((bf16[64,2176]{1,0:T(8,128)(2,1)S(1)}, bf16[64,2176]{1,0:T(8,128)(2,1)S(1)}, u32[]{:S(2)}, u32[]{:S(2)}) %collective-permute-start.5) | collective-permute-done | bytes 278560 | tf_op jit(solution)/shard_map/ppermute | solution.py:292
  24.4 0.4 collective-permute-start.6
  24.8 1.8 %shard_map.71.refs_4_ = f32[64,2048]{1,0:T(8,128)S(1)} custom-call(bf16[64,2176]{1,0:T(8,128)(2,1)S(1)} %collective-permute-done.2.refs_0_, bf16[1,2048,768]{2,1,0:T(8,128)(2,1)S(1)} %get-tuple-element.49.refs_1_.refs_2_, bf16[1,2048,768]{2,1,0:T(8,128)(2,1)S(1)} %get-tuple-element.50.refs_2_.refs_3_, bf16[1,768,2048]{2,1,0:T(8,128)(2,1)S(1)} %get-tuple-element.51.refs_3_.refs_4_), custom_call_target="tpu_custom_call" | custom-call | flops 603979776 | bytes 9961472 | tf_op jit(solution)/shard_map/pallas_call | solution.py:139
  26.6 1.8 %shard_map.70.refs_4_ = f32[64,2048]{1,0:T(8,128)S(1)} custom-call(bf16[64,2176]{1,0:T(8,128)(2,1)S(1)} %collective-permute-done.5.refs_0_, bf16[1,2048,768]{2,1,0:T(8,128)(2,1)S(1)} %get-tuple-element.49.refs_1_.refs_2_, bf16[1,2048,768]{2,1,0:T(8,128)(2,1)S(1)} %get-tuple-element.50.refs_2_.refs_3_, bf16[1,768,2048]{2,1,0:T(8,128)(2,1)S(1)} %get-tuple-element.51.refs_3_.refs_4_), custom_call_target="tpu_custom_call" | custom-call | flops 603979776 | bytes 9961472 | tf_op jit(solution)/shard_map/pallas_call | solution.py:139
  28.4 0.5 collective-permute-done.4.refs_0_
  28.9 3.2 %collective-permute-done.6.refs_1_ = bf16[64,2176]{1,0:T(8,128)(2,1)S(1)} collective-permute-done((bf16[64,2176]{1,0:T(8,128)(2,1)S(1)}, bf16[64,2176]{1,0:T(8,128)(2,1)S(1)}, u32[]{:S(2)}, u32[]{:S(2)}) %collective-permute-start.6) | collective-permute-done | bytes 278560 | tf_op jit(solution)/shard_map/ppermute | solution.py:292
  32.1 0.0 collective-permute-done.7.refs_5_.refs_1_
  32.1 0.0 collective-permute-done.8.refs_6_.refs_2_
  32.2 0.0 collective-permute-done.9.refs_7_.refs_3_
  32.2 2.8 %shard_map.72 = (f32[64,2048]{1,0:T(8,128)S(1)}, f32[64,2048]{1,0:T(8,128)S(1)}) custom-call(bf16[64,2176]{1,0:T(8,128)(2,1)S(1)} %collective-permute-done.4.refs_0_, bf16[64,2176]{1,0:T(8,128)(2,1)S(1)} %collective-permute-done.6.refs_1_, bf16[1,2048,768]{2,1,0:T(8,128)(2,1)S(1)} %get-tuple-element.49.refs_1_.refs_2_, ...), custom_call_target="tpu_custom_call" | custom-call | flops 2415919104 | bytes 19922944 | tf_op jit(solution)/shard_map/pallas_call | solution.py:139
  35.0 1.1 %collective-permute-start.11 = (bf16[64,2048]{1,0:T(8,128)(2,1)S(1)}, bf16[64,2048]{1,0:T(8,128)(2,1)S(1)}, u32[]{:S(2)}, u32[]{:S(2)}) collective-permute-start(bf16[64,2048]{1,0:T(8,128)(2,1)S(1)} %convert_element_type.45), channel_id=1, source_target_pairs={{0,5},{1,2},{2,7},{3,0},{6,3},{7,10},{10,15},{11,6},{14,11},{15,12... | collective-permute-start | bytes 786440 | tf_op jit(solution)/shard_map/ppermute | solution.py:295
  36.1 1.8 %shard_map.73 = f32[64,2048]{1,0:T(8,128)S(1)} custom-call(bf16[64,2176]{1,0:T(8,128)(2,1)S(1)} %collective-permute-done.5.refs_0_, bf16[1,2048,768]{2,1,0:T(8,128)(2,1)S(1)} %collective-permute-done.7.refs_5_.refs_1_, bf16[1,2048,768]{2,1,0:T(8,128)(2,1)S(1)} %collective-permute-done.8.refs_6_.refs_2_, ...), custom_call_target="tpu_custom_call" | custom-call | flops 603979776 | bytes 9961472 | tf_op jit(solution)/shard_map/pallas_call | solution.py:139
  37.9 1.8 %shard_map.74 = f32[64,2048]{1,0:T(8,128)S(1)} custom-call(bf16[64,2176]{1,0:T(8,128)(2,1)S(1)} %collective-permute-done.2.refs_0_, bf16[1,2048,768]{2,1,0:T(8,128)(2,1)S(1)} %collective-permute-done.7.refs_5_.refs_1_, bf16[1,2048,768]{2,1,0:T(8,128)(2,1)S(1)} %collective-permute-done.8.refs_6_.refs_2_, ...), custom_call_target="tpu_custom_call" | custom-call | flops 603979776 | bytes 9961472 | tf_op jit(solution)/shard_map/pallas_call | solution.py:139
  39.8 0.9 %collective-permute-start.10 = (bf16[64,2048]{1,0:T(8,128)(2,1)S(1)}, bf16[64,2048]{1,0:T(8,128)(2,1)S(1)}, u32[]{:S(2)}, u32[]{:S(2)}) collective-permute-start(bf16[64,2048]{1,0:T(8,128)(2,1)S(1)} %convert_element_type.46), channel_id=1, source_target_pairs={{0,3},{1,4},{2,1},{3,6},{6,11},{7,2},{10,7},{11,14},{14,13},{15,10... | collective-permute-start | bytes 786440 | tf_op jit(solution)/shard_map/ppermute | solution.py:295
  40.7 0.3 collective-permute-done.11
  41.1 0.9 %collective-permute-start.13 = (bf16[64,2048]{1,0:T(8,128)(2,1)S(1)}, bf16[64,2048]{1,0:T(8,128)(2,1)S(1)}, u32[]{:S(2)}, u32[]{:S(2)}) collective-permute-start(bf16[64,2048]{1,0:T(8,128)(2,1)S(1)} %add_convert_fusion.5), channel_id=1, source_target_pairs={{0,5},{1,2},{2,7},{3,0},{6,3},{7,10},{10,15},{11,6},{14,11},{15,12... | collective-permute-start | bytes 786440 | tf_op jit(solution)/shard_map/ppermute | solution.py:295
  42.0 1.8 %shard_map.75 = f32[64,2048]{1,0:T(8,128)S(1)} custom-call(bf16[64,2176]{1,0:T(8,128)(2,1)S(1)} %collective-permute-done.3.refs_0_, bf16[1,2048,768]{2,1,0:T(8,128)(2,1)S(1)} %collective-permute-done.7.refs_5_.refs_1_, bf16[1,2048,768]{2,1,0:T(8,128)(2,1)S(1)} %collective-permute-done.8.refs_6_.refs_2_, ...), custom_call_target="tpu_custom_call" | custom-call | flops 603979776 | bytes 9961472 | tf_op jit(solution)/shard_map/pallas_call | solution.py:139
  43.8 1.8 %shard_map.76 = f32[64,2048]{1,0:T(8,128)S(1)} custom-call(bf16[64,2176]{1,0:T(8,128)(2,1)S(1)} %collective-permute-done.refs_0_, bf16[1,2048,768]{2,1,0:T(8,128)(2,1)S(1)} %collective-permute-done.7.refs_5_.refs_1_, bf16[1,2048,768]{2,1,0:T(8,128)(2,1)S(1)} %collective-permute-done.8.refs_6_.refs_2_, ...), custom_call_target="tpu_custom_call" | custom-call | flops 603979776 | bytes 9961472 | tf_op jit(solution)/shard_map/pallas_call | solution.py:139
  45.6 1.8 %collective-permute-done.10 = bf16[64,2048]{1,0:T(8,128)(2,1)S(1)} collective-permute-done((bf16[64,2048]{1,0:T(8,128)(2,1)S(1)}, bf16[64,2048]{1,0:T(8,128)(2,1)S(1)}, u32[]{:S(2)}, u32[]{:S(2)}) %collective-permute-start.10) | collective-permute-done | bytes 262176 | tf_op jit(solution)/shard_map/ppermute | solution.py:295
  47.5 0.1 add_convert_fusion.4
  47.5 0.7 %collective-permute-start.12 = (bf16[64,2048]{1,0:T(8,128)(2,1)S(1)}, bf16[64,2048]{1,0:T(8,128)(2,1)S(1)}, u32[]{:S(2)}, u32[]{:S(2)}) collective-permute-start(bf16[64,2048]{1,0:T(8,128)(2,1)S(1)} %add_convert_fusion.4), channel_id=1, source_target_pairs={{0,3},{1,4},{2,1},{3,6},{6,11},{7,2},{10,7},{11,14},{14,13},{15,10... | collective-permute-start | bytes 786440 | tf_op jit(solution)/shard_map/ppermute | solution.py:295
  48.3 1.1 %collective-permute-done.13 = bf16[64,2048]{1,0:T(8,128)(2,1)S(1)} collective-permute-done((bf16[64,2048]{1,0:T(8,128)(2,1)S(1)}, bf16[64,2048]{1,0:T(8,128)(2,1)S(1)}, u32[]{:S(2)}, u32[]{:S(2)}) %collective-permute-start.13) | collective-permute-done | bytes 262176 | tf_op jit(solution)/shard_map/ppermute | solution.py:295
  49.4 0.6 collective-permute-start.14
  50.1 1.8 %shard_map.77 = f32[64,2048]{1,0:T(8,128)S(1)} custom-call(bf16[64,2176]{1,0:T(8,128)(2,1)S(1)} %collective-permute-done.1.refs_0_, bf16[1,2048,768]{2,1,0:T(8,128)(2,1)S(1)} %collective-permute-done.7.refs_5_.refs_1_, bf16[1,2048,768]{2,1,0:T(8,128)(2,1)S(1)} %collective-permute-done.8.refs_6_.refs_2_, ...), custom_call_target="tpu_custom_call" | custom-call | flops 603979776 | bytes 9961472 | tf_op jit(solution)/shard_map/pallas_call | solution.py:139
  51.9 1.8 %shard_map.78 = f32[64,2048]{1,0:T(8,128)S(1)} custom-call(bf16[64,2176]{1,0:T(8,128)(2,1)S(1)} %shard_map.64.rows_ref.refs_0_, bf16[1,2048,768]{2,1,0:T(8,128)(2,1)S(1)} %collective-permute-done.7.refs_5_.refs_1_, bf16[1,2048,768]{2,1,0:T(8,128)(2,1)S(1)} %collective-permute-done.8.refs_6_.refs_2_, ...), custom_call_target="tpu_custom_call" | custom-call | flops 603979776 | bytes 9961472 | tf_op jit(solution)/shard_map/pallas_call | solution.py:139
  53.7 1.6 %collective-permute-done.12 = bf16[64,2048]{1,0:T(8,128)(2,1)S(1)} collective-permute-done((bf16[64,2048]{1,0:T(8,128)(2,1)S(1)}, bf16[64,2048]{1,0:T(8,128)(2,1)S(1)}, u32[]{:S(2)}, u32[]{:S(2)}) %collective-permute-start.12) | collective-permute-done | bytes 262176 | tf_op jit(solution)/shard_map/ppermute | solution.py:295
  55.3 0.1 add_convert_fusion.1
  55.4 0.1 collective-permute-start.16
  55.4 2.6 %collective-permute-done.14 = bf16[64,2048]{1,0:T(8,128)(2,1)S(1)} collective-permute-done((bf16[64,2048]{1,0:T(8,128)(2,1)S(1)}, bf16[64,2048]{1,0:T(8,128)(2,1)S(1)}, u32[]{:S(2)}, u32[]{:S(2)}) %collective-permute-start.14) | collective-permute-done | bytes 262176 | tf_op jit(solution)/shard_map/ppermute | solution.py:295
  58.1 0.1 add_convert_fusion.2
  58.1 0.4 collective-permute-start.15
  58.5 4.6 %collective-permute-done.16 = bf16[64,2048]{1,0:T(8,128)(2,1)S(1)} collective-permute-done((bf16[64,2048]{1,0:T(8,128)(2,1)S(1)}, bf16[64,2048]{1,0:T(8,128)(2,1)S(1)}, u32[]{:S(2)}, u32[]{:S(2)}) %collective-permute-start.16) | collective-permute-done | bytes 262176 | tf_op jit(solution)/shard_map/ppermute | solution.py:295
  63.1 3.4 %collective-permute-done.15 = bf16[64,2048]{1,0:T(8,128)(2,1)S(1)} collective-permute-done((bf16[64,2048]{1,0:T(8,128)(2,1)S(1)}, bf16[64,2048]{1,0:T(8,128)(2,1)S(1)}, u32[]{:S(2)}, u32[]{:S(2)}) %collective-permute-start.15) | collective-permute-done | bytes 262176 | tf_op jit(solution)/shard_map/ppermute | solution.py:295
  66.5 0.8 %add_convert_fusion = bf16[64,2048]{1,0:T(8,128)(2,1)} fusion(bf16[64,2048]{1,0:T(8,128)(2,1)S(1)} %collective-permute-done.16, f32[64,2048]{1,0:T(8,128)S(1)} %shard_map.78, bf16[64,2048]{1,0:T(8,128)(2,1)S(1)} %collective-permute-done.15), kind=kLoop, calls=%fused_computation | loop fusion | flops 655360 | bytes 1310720 | tf_op jit(solution)/shard_map/convert_element_type | solution.py:273
  (4 shorter events, 0.2 us)
Async XLA Ops:
  1.0 31.1 %collective-permute-start.7 = (bf16[1,2048,768]{2,1,0:T(8,128)(2,1)}, bf16[1,2048,768]{2,1,0:T(8,128)(2,1)S(1)}, u32[]{:S(2)}, u32[]{:S(2)}) collective-permute-start(bf16[1,2048,768]{2,1,0:T(8,128)(2,1)} %gate_in.1), channel_id=1, source_target_pairs={{0,1},{1,0},{2,3},{3,2},{4,5},{5,4},{6,7},{7,6},{8,9},{9,8},{10,11... | collective-permute-start | bytes 9437192 | tf_op jit(solution)/shard_map/ppermute | solution.py:299
  1.5 30.6 %collective-permute-start.8 = (bf16[1,2048,768]{2,1,0:T(8,128)(2,1)}, bf16[1,2048,768]{2,1,0:T(8,128)(2,1)S(1)}, u32[]{:S(2)}, u32[]{:S(2)}) collective-permute-start(bf16[1,2048,768]{2,1,0:T(8,128)(2,1)} %up_in.1), channel_id=1, source_target_pairs={{0,1},{1,0},{2,3},{3,2},{4,5},{5,4},{6,7},{7,6},{8,9},{9,8},{10,11... | collective-permute-start | bytes 9437192 | tf_op jit(solution)/shard_map/ppermute | solution.py:299
  1.6 30.5 %collective-permute-start.9 = (bf16[1,768,2048]{2,1,0:T(8,128)(2,1)}, bf16[1,768,2048]{2,1,0:T(8,128)(2,1)S(1)}, u32[]{:S(2)}, u32[]{:S(2)}) collective-permute-start(bf16[1,768,2048]{2,1,0:T(8,128)(2,1)} %down_in.1), channel_id=1, source_target_pairs={{0,1},{1,0},{2,3},{3,2},{4,5},{5,4},{6,7},{7,6},{8,9},{9,8},{10,11... | collective-permute-start | bytes 9437192 | tf_op jit(solution)/shard_map/ppermute | solution.py:299
  2.0 8.2 %collective-permute-start.1 = (bf16[64,2176]{1,0:T(8,128)(2,1)S(1)}, bf16[64,2176]{1,0:T(8,128)(2,1)S(1)}, u32[]{:S(2)}, u32[]{:S(2)}) collective-permute-start(bf16[64,2176]{1,0:T(8,128)(2,1)S(1)} %shard_map.64.rows_ref.refs_0_), channel_id=1, source_target_pairs={{0,3},{1,4},{2,1},{3,6},{6,11},{7,2},{10,7},{11,14},{14,13},{15,10... | collective-permute-start | bytes 835592 | tf_op jit(solution)/shard_map/ppermute | solution.py:292
  7.9 6.4 %collective-permute-start = (bf16[64,2176]{1,0:T(8,128)(2,1)S(1)}, bf16[64,2176]{1,0:T(8,128)(2,1)S(1)}, u32[]{:S(2)}, u32[]{:S(2)}) collective-permute-start(bf16[64,2176]{1,0:T(8,128)(2,1)S(1)} %shard_map.64.rows_ref.refs_0_), channel_id=1, source_target_pairs={{0,5},{1,2},{2,7},{3,0},{6,3},{7,10},{10,15},{11,6},{14,11},{15,12... | collective-permute-start | bytes 835592 | tf_op jit(solution)/shard_map/ppermute | solution.py:292
  10.2 7.0 %collective-permute-start.3 = (bf16[64,2176]{1,0:T(8,128)(2,1)S(1)}, bf16[64,2176]{1,0:T(8,128)(2,1)S(1)}, u32[]{:S(2)}, u32[]{:S(2)}) collective-permute-start(bf16[64,2176]{1,0:T(8,128)(2,1)S(1)} %collective-permute-done.1.refs_0_), channel_id=1, source_target_pairs={{0,3},{1,4},{2,1},{3,6},{6,11},{7,2},{10,7},{11,14},{14,13},{15,10... | collective-permute-start | bytes 835592 | tf_op jit(solution)/shard_map/ppermute | solution.py:292
  14.3 7.9 %collective-permute-start.2 = (bf16[64,2176]{1,0:T(8,128)(2,1)S(1)}, bf16[64,2176]{1,0:T(8,128)(2,1)S(1)}, u32[]{:S(2)}, u32[]{:S(2)}) collective-permute-start(bf16[64,2176]{1,0:T(8,128)(2,1)S(1)} %collective-permute-done.refs_0_), channel_id=1, source_target_pairs={{0,5},{1,2},{2,7},{3,0},{6,3},{7,10},{10,15},{11,6},{14,11},{15,12... | collective-permute-start | bytes 835592 | tf_op jit(solution)/shard_map/ppermute | solution.py:292
  17.3 7.2 %collective-permute-start.5 = (bf16[64,2176]{1,0:T(8,128)(2,1)S(1)}, bf16[64,2176]{1,0:T(8,128)(2,1)S(1)}, u32[]{:S(2)}, u32[]{:S(2)}) collective-permute-start(bf16[64,2176]{1,0:T(8,128)(2,1)S(1)} %collective-permute-done.3.refs_0_), channel_id=1, source_target_pairs={{0,3},{1,4},{2,1},{3,6},{6,11},{7,2},{10,7},{11,14},{14,13},{15,10... | collective-permute-start | bytes 835592 | tf_op jit(solution)/shard_map/ppermute | solution.py:292
  22.2 6.8 %collective-permute-start.4 = (bf16[64,2176]{1,0:T(8,128)(2,1)S(1)}, bf16[64,2176]{1,0:T(8,128)(2,1)S(1)}, u32[]{:S(2)}, u32[]{:S(2)}) collective-permute-start(bf16[64,2176]{1,0:T(8,128)(2,1)S(1)} %collective-permute-done.2.refs_0_), channel_id=1, source_target_pairs={{0,5},{1,2},{2,7},{3,0},{6,3},{7,10},{10,15},{11,6},{14,11},{15,12... | collective-permute-start | bytes 835592 | tf_op jit(solution)/shard_map/ppermute | solution.py:292
  24.4 7.7 %collective-permute-start.6 = (bf16[64,2176]{1,0:T(8,128)(2,1)S(1)}, bf16[64,2176]{1,0:T(8,128)(2,1)S(1)}, u32[]{:S(2)}, u32[]{:S(2)}) collective-permute-start(bf16[64,2176]{1,0:T(8,128)(2,1)S(1)} %collective-permute-done.5.refs_0_), channel_id=1, source_target_pairs={{0,3},{1,4},{2,1},{3,6},{6,11},{7,2},{10,7},{11,14},{14,13},{15,10... | collective-permute-start | bytes 835592 | tf_op jit(solution)/shard_map/ppermute | solution.py:292
  35.0 6.0 %collective-permute-start.11 = (bf16[64,2048]{1,0:T(8,128)(2,1)S(1)}, bf16[64,2048]{1,0:T(8,128)(2,1)S(1)}, u32[]{:S(2)}, u32[]{:S(2)}) collective-permute-start(bf16[64,2048]{1,0:T(8,128)(2,1)S(1)} %convert_element_type.45), channel_id=1, source_target_pairs={{0,5},{1,2},{2,7},{3,0},{6,3},{7,10},{10,15},{11,6},{14,11},{15,12... | collective-permute-start | bytes 786440 | tf_op jit(solution)/shard_map/ppermute | solution.py:295
  39.8 7.7 %collective-permute-start.10 = (bf16[64,2048]{1,0:T(8,128)(2,1)S(1)}, bf16[64,2048]{1,0:T(8,128)(2,1)S(1)}, u32[]{:S(2)}, u32[]{:S(2)}) collective-permute-start(bf16[64,2048]{1,0:T(8,128)(2,1)S(1)} %convert_element_type.46), channel_id=1, source_target_pairs={{0,3},{1,4},{2,1},{3,6},{6,11},{7,2},{10,7},{11,14},{14,13},{15,10... | collective-permute-start | bytes 786440 | tf_op jit(solution)/shard_map/ppermute | solution.py:295
  41.1 8.3 %collective-permute-start.13 = (bf16[64,2048]{1,0:T(8,128)(2,1)S(1)}, bf16[64,2048]{1,0:T(8,128)(2,1)S(1)}, u32[]{:S(2)}, u32[]{:S(2)}) collective-permute-start(bf16[64,2048]{1,0:T(8,128)(2,1)S(1)} %add_convert_fusion.5), channel_id=1, source_target_pairs={{0,5},{1,2},{2,7},{3,0},{6,3},{7,10},{10,15},{11,6},{14,11},{15,12... | collective-permute-start | bytes 786440 | tf_op jit(solution)/shard_map/ppermute | solution.py:295
  47.5 7.8 %collective-permute-start.12 = (bf16[64,2048]{1,0:T(8,128)(2,1)S(1)}, bf16[64,2048]{1,0:T(8,128)(2,1)S(1)}, u32[]{:S(2)}, u32[]{:S(2)}) collective-permute-start(bf16[64,2048]{1,0:T(8,128)(2,1)S(1)} %add_convert_fusion.4), channel_id=1, source_target_pairs={{0,3},{1,4},{2,1},{3,6},{6,11},{7,2},{10,7},{11,14},{14,13},{15,10... | collective-permute-start | bytes 786440 | tf_op jit(solution)/shard_map/ppermute | solution.py:295
  49.4 8.6 %collective-permute-start.14 = (bf16[64,2048]{1,0:T(8,128)(2,1)S(1)}, bf16[64,2048]{1,0:T(8,128)(2,1)S(1)}, u32[]{:S(2)}, u32[]{:S(2)}) collective-permute-start(bf16[64,2048]{1,0:T(8,128)(2,1)S(1)} %add_convert_fusion.3), channel_id=1, source_target_pairs={{0,5},{1,2},{2,7},{3,0},{6,3},{7,10},{10,15},{11,6},{14,11},{15,12... | collective-permute-start | bytes 786440 | tf_op jit(solution)/shard_map/ppermute | solution.py:295
  55.4 7.8 %collective-permute-start.16 = (bf16[64,2048]{1,0:T(8,128)(2,1)S(1)}, bf16[64,2048]{1,0:T(8,128)(2,1)S(1)}, u32[]{:S(2)}, u32[]{:S(2)}) collective-permute-start(bf16[64,2048]{1,0:T(8,128)(2,1)S(1)} %add_convert_fusion.1), channel_id=1, source_target_pairs={{0,3},{1,4},{2,1},{3,6},{6,11},{7,2},{10,7},{11,14},{14,13},{15,10... | collective-permute-start | bytes 786440 | tf_op jit(solution)/shard_map/ppermute | solution.py:295
  58.1 8.4 %collective-permute-start.15 = (bf16[64,2048]{1,0:T(8,128)(2,1)S(1)}, bf16[64,2048]{1,0:T(8,128)(2,1)S(1)}, u32[]{:S(2)}, u32[]{:S(2)}) collective-permute-start(bf16[64,2048]{1,0:T(8,128)(2,1)S(1)} %add_convert_fusion.2), channel_id=1, source_target_pairs={{0,5},{1,2},{2,7},{3,0},{6,3},{7,10},{10,15},{11,6},{14,11},{15,12... | collective-permute-start | bytes 786440 | tf_op jit(solution)/shard_map/ppermute | solution.py:295
